TPU v7x, 32 devices: a whole 2x2x4 slice. The times are simulated.
32 devices in a mesh: parts: 2 (over x), wide: 16 (over z, y, core).
Axes of the slice: x: 2, y: 2, z: 4, core: 2. Of those that a mesh axis runs over, the one named last changes fastest.
Arguments:
- a_rows: bfloat16 [40960, 2048], P(('parts', 'wide')), parts along dimension 0, may hold values from -6 to 6
- xa_panel: bfloat16 [4096, 256], P(('parts', 'wide')), parts along dimension 0, may hold values from -0.125 to 0.125
- za_panel: bfloat16 [4096, 256], P(('parts', 'wide')), parts along dimension 0, may hold values from -0.125 to 0.125
- send_order: int32 [32, 1280], P(('parts', 'wide')), parts along dimension 0, may hold values from 0 to 1279, each once within a row
- recv_order: int32 [32, 1280], P(('parts', 'wide')), parts along dimension 0, may hold values from 0 to 1279, each once within a row
- shift: float32 [128], P('parts'), parts along dimension 0, may hold values from 1 to 8
- resident: bfloat16 [40960, 1024], P(('parts', 'wide')), parts along dimension 0, may hold values from -6 to 6
Outputs:
- factored: float32 [40960, 256], P(('parts', 'wide')), parts along dimension 0
- updated: bfloat16 [40960, 1024], P(('parts', 'wide')), parts along dimension 0
- pivots: float32 [128], P('parts'), parts along dimension 0
There are 2 independent parts, one for each index of `parts`. A program takes and returns all parts, laid end to end along the dimension named above; each array names one. Nothing has to cross between parts.
Inputs may be any that keep to these rules, and one draw needn't show every extreme that they name: Each row of send_order is a permutation of the local constraint rows. Each row of recv_order is a permutation of the received slots.
All inputs are finite; a program needn't handle non-finite values.
Results may differ from a plain program's by a relative error of at most 0.0004.
Values may be sent and summed in bfloat16 or wider, within the bound.
No kernel may reach another device: no remote copies, remote signals or barrier semaphores. Data moves between devices by JAX's collectives and lax.ppermute only.
A program may use at most 64 MiB of HBM per device.

v0:
```python
import functools

import jax
import jax.numpy as jnp
from jax import lax
from jax.experimental import pallas as pl
from jax.experimental.pallas import tpu as pltpu
from jax.sharding import PartitionSpec as P

PANEL = 64
LANES = 128
A_BLOCK = 640
DEEP_BLOCK = 256
F32 = jnp.float32
BF16 = jnp.bfloat16
MIB = 1024 * 1024


def params(mebibytes=12):
    return pltpu.CompilerParams(vmem_limit_bytes=mebibytes * MIB)


def in_hbm(x):
    return pltpu.with_memory_space_constraint(x, pltpu.HBM)


def lane_ids(shape):
    return lax.broadcasted_iota(jnp.int32, shape, len(shape) - 1)


def split(x, count):
    terms = []
    for _ in range(count):
        term = x.astype(BF16)
        terms.append(term)
        x = x - term.astype(F32)
    return terms


def swap_halves(x):
    return pltpu.roll(x, LANES // 2, 1)


def as_column(index_row):
    return jnp.transpose(jnp.broadcast_to(index_row, (LANES, LANES)))


def picks_of(at, width):
    lanes = lane_ids(at.shape)
    return jnp.concatenate(
        [(at == lanes + column).astype(F32).astype(BF16) for column in range(0, width, LANES)], axis=1
    )


def fill_picks(at_ref, picks_ref):
    rows, width = picks_ref.shape
    for start in range(0, rows, LANES):
        picks_ref[start : start + LANES, :] = picks_of(at_ref[start : start + LANES, :], width)


def one_hot(index_row, width):
    chunks = [
        picks_of(as_column(index_row[:, start : start + LANES]), width)
        for start in range(0, index_row.shape[1], LANES)
    ]
    return jnp.concatenate(chunks, axis=0) if len(chunks) > 1 else chunks[0]


def packed_order(share, half, slot):
    part = share // 2
    return (slot % share) // part * half + slot // share * part + slot % part


def fill_order(order_ref, at_ref, share):
    rows = order_ref.shape[1]
    height = 8
    for start in range(0, rows, LANES):
        column = as_column(order_ref[:, start : start + LANES])
        if not share:
            at_ref[start : start + LANES, :] = column
            continue
        for inner in range(0, LANES, height):
            place = packed_order(share, rows // 2, start + inner)
            at_ref[place : place + height, :] = column[inner : inner + height]


def exchange(held, masks, axis):
    size = lax.axis_size(axis)
    combined = [0]
    for mask in masks:
        combined += [other ^ mask for other in combined]
    parts = list(held)
    for mask in combined[1:]:
        parts += [lax.ppermute(part, axis, [(i, i ^ mask) for i in range(size)]) for part in held]
    return parts


def offsets_of(phases):
    offsets = [0]
    for masks in phases:
        combined = [0]
        for mask in masks:
            combined += [other ^ mask for other in combined]
        offsets = [offset ^ mask for mask in combined for offset in offsets]
    return offsets


def join(parts):
    return [jnp.concatenate(parts, axis=0)]


def phases_of(size):
    bits = [1 << bit for bit in reversed(range(size.bit_length() - 1))]
    return [bits[start : start + 2] for start in range(0, len(bits), 2)], [[bit] for bit in bits]


def tied(parts, *earlier):
    return list(lax.optimization_barrier((*parts, *earlier))[: len(parts)])


def picks_kernel(share, order_hbm, a_hbm, picks_ref, copy_ref, order_ref, at_ref, sems):
    fetch = pltpu.make_async_copy(order_hbm, order_ref, sems.at[0])
    copy = pltpu.make_async_copy(a_hbm, copy_ref, sems.at[1])
    fetch.start()
    copy.start()
    fetch.wait()
    fill_order(order_ref, at_ref, share)
    fill_picks(at_ref, picks_ref)
    copy.wait()


def order_picks(order, a_rows, share):
    rows, depth = a_rows.shape
    return pl.pallas_call(
        functools.partial(picks_kernel, share),
        in_specs=[pl.BlockSpec(memory_space=pltpu.HBM)] * 2,
        out_specs=[pl.BlockSpec(memory_space=pltpu.VMEM)] * 2,
        out_shape=[jax.ShapeDtypeStruct((rows, rows), BF16), jax.ShapeDtypeStruct((rows, depth), BF16)],
        scratch_shapes=[
            pltpu.VMEM((1, rows), jnp.int32),
            pltpu.VMEM((rows, LANES), jnp.int32),
            pltpu.SemaphoreType.DMA((2,)),
        ],
        compiler_params=params(),
        cost_estimate=pl.CostEstimate(flops=4 * rows * rows, bytes_accessed=4 * rows * depth, transcendentals=0),
        name="order_picks",
    )(in_hbm(order), in_hbm(a_rows))


def panels_kernel(my_ref, xa_hbm, za_hbm, lead_ref, rest_ref, xa_ref, za_ref, sems):
    copies = [
        pltpu.make_async_copy(xa_hbm, xa_ref, sems.at[0]),
        pltpu.make_async_copy(za_hbm, za_ref, sems.at[1]),
    ]
    for copy in copies:
        copy.start()
    for copy in copies:
        copy.wait()
    lead_ref[0] = jnp.concatenate([xa_ref[:, :PANEL], za_ref[:, :PANEL]], axis=1)
    rest_ref[0, :, :LANES] = jnp.concatenate([xa_ref[:, PANEL:LANES], za_ref[:, PANEL:LANES]], axis=1)
    rest_ref[0, :, LANES : 2 * LANES] = xa_ref[:, LANES:]
    rest_ref[0, :, 2 * LANES :] = za_ref[:, LANES:]


def split_panels(my_index, xa_panel, za_panel):
    depth, columns = xa_panel.shape
    return pl.pallas_call(
        panels_kernel,
        in_specs=[pl.BlockSpec(memory_space=pltpu.SMEM)] + [pl.BlockSpec(memory_space=pltpu.HBM)] * 2,
        out_shape=[
            jax.ShapeDtypeStruct((1, depth, LANES), BF16),
            jax.ShapeDtypeStruct((1, depth, 2 * columns - LANES), BF16),
        ],
        scratch_shapes=[
            pltpu.VMEM((depth, columns), BF16),
            pltpu.VMEM((depth, columns), BF16),
            pltpu.SemaphoreType.DMA((2,)),
        ],
        compiler_params=params(),
        name="split_panels",
    )(my_index, in_hbm(xa_panel), in_hbm(za_panel))


def assemble(my_index, offsets, parts, panel_ref):
    position = 0
    for part in parts:
        for number in range(part.shape[0]):
            depth = part.shape[1]
            start = pl.multiple_of((my_index ^ offsets[position]) * depth, depth)
            panel_ref[pl.ds(start, depth), :] = part[number]
            position += 1


def whole_sum(got):
    pair = got[:, :LANES]
    return (pair + swap_halves(pair)) + got[:, LANES:]


def lead_product_kernel(offsets, my_ref, a_ref, picks_ref, *refs):
    parts, (out_ref, panel_ref, terms_ref) = refs[:-3], refs[-3:]
    assemble(my_ref[0], offsets, parts, panel_ref)
    rows = a_ref.shape[0]
    for start in range(0, rows, DEEP_BLOCK):
        both = jnp.dot(a_ref[start : start + DEEP_BLOCK, :], panel_ref[...], preferred_element_type=F32)
        first, second, third = (term.astype(F32) for term in split(both * swap_halves(both), 3))
        near = lane_ids(both.shape) < PANEL
        terms_ref[start : start + DEEP_BLOCK, :LANES] = jnp.where(near, first, second).astype(BF16)
        terms_ref[start : start + DEEP_BLOCK, LANES:] = third.astype(BF16)
    half = rows // 2
    block = half // 2
    for start in range(0, half, block):
        low = jnp.dot(picks_ref[start : start + block, :], terms_ref[...], preferred_element_type=F32)
        high = jnp.dot(picks_ref[half + start : half + start + block, :], terms_ref[...], preferred_element_type=F32)
        low, high = whole_sum(low), whole_sum(high)
        out_ref[start : start + block, :] = jnp.where(lane_ids(low.shape) < PANEL, low, high)


def lead_products(my_index, a_rows, picks, parts, offsets):
    rows, depth = a_rows.shape
    return pl.pallas_call(
        functools.partial(lead_product_kernel, offsets),
        in_specs=[pl.BlockSpec(memory_space=pltpu.SMEM)] + [pl.BlockSpec(memory_space=pltpu.VMEM)] * (2 + len(parts)),
        out_specs=pl.BlockSpec(memory_space=pltpu.VMEM),
        out_shape=jax.ShapeDtypeStruct((rows // 2, LANES), F32),
        scratch_shapes=[pltpu.VMEM((depth, LANES), BF16), pltpu.VMEM((rows, 2 * LANES), BF16)],
        compiler_params=params(),
        cost_estimate=pl.CostEstimate(
            flops=2 * rows * (depth + 2 * rows) * LANES, bytes_accessed=2 * rows * depth, transcendentals=0
        ),
        name="lead_products",
    )(my_index, a_rows, picks, *parts)


BIAS = 128
MARGIN = 0.9995
ROUNDER = 1.5 * 2.0**23


def nearest(x):
    return (x + ROUNDER) - ROUNDER


def rest_product_kernel(offsets, share, my_ref, order_ref, a_hbm, *refs):
    parts, (out_ref, a_ref, at_ref, picks_ref, panel_ref, terms_ref, sems) = refs[:-7], refs[-7:]
    rows = a_ref.shape[0]
    half = rows // 2
    block = DEEP_BLOCK
    starts = range(0, rows, block)
    copies = [
        pltpu.make_async_copy(a_hbm.at[pl.ds(start, block), :], a_ref.at[pl.ds(start, block), :], sems.at[i])
        for i, start in enumerate(starts)
    ]
    for copy in copies[:3]:
        copy.start()
    assemble(my_ref[0], offsets, parts, panel_ref)
    fill_order(order_ref, at_ref, share)
    fill_picks(at_ref, picks_ref)

    def product(i):
        copies[i].wait()
        if i + 3 < len(copies):
            copies[i + 3].start()
        return jnp.dot(a_ref[starts[i] : starts[i] + block, :], panel_ref[...], preferred_element_type=F32)

    low_lanes = lane_ids((block, LANES)) < PANEL
    later = product(0)
    for i, start in enumerate(starts):
        both = later
        if i + 1 < len(starts):
            later = product(i + 1)
        near = both[:, :LANES]
        near = near * swap_halves(near)
        far = both[:, LANES : 2 * LANES] * both[:, 2 * LANES :]
        largest = jnp.max(jnp.maximum(jnp.abs(near), jnp.abs(far)), axis=1, keepdims=True)
        exponent = jnp.floor(jnp.log2(jnp.maximum(largest, 1e-30))) + 1.0
        scale = jnp.exp2(15.0 - exponent) * MARGIN
        far = nearest(far * scale)
        near = nearest(near * scale)
        far_top = nearest(far * (1 / 256))
        near_top = nearest(near * (1 / 256))
        here = slice(start, start + block)
        terms_ref[here, :LANES] = far_top.astype(BF16)
        terms_ref[here, LANES : 2 * LANES] = (far - far_top * 256.0).astype(BF16)
        terms_ref[here, 2 * LANES : 3 * LANES] = jnp.where(low_lanes, near_top, near - near_top * 256.0).astype(BF16)
        terms_ref[here, 3 * LANES :] = jnp.broadcast_to(exponent, (block, LANES)).astype(BF16)

    def coded(start, size):
        got = jnp.dot(picks_ref[start : start + size, :], terms_ref[...], preferred_element_type=F32)
        far = got[:, :LANES] * 256.0 + got[:, LANES : 2 * LANES]
        pair = got[:, 2 * LANES : 3 * LANES]
        pair = jnp.where(lane_ids(pair.shape) < PANEL, pair * 256.0, pair)
        near = (pair + swap_halves(pair)).astype(jnp.int32) * 65536 + (got[:, 3 * LANES :].astype(jnp.int32) + BIAS)
        return far.astype(jnp.int32), near

    block = half // 2
    for start in range(0, half, block):
        far_low, near_low = coded(start, block)
        far_high, near_high = coded(half + start, block)
        out_ref[start : start + block, :LANES] = far_low * 65536 + (far_high & 65535)
        out_ref[start : start + block, LANES:] = jnp.where(lane_ids(near_low.shape) < PANEL, near_low, near_high)


def rest_products(my_index, order, a_rows, parts, offsets, share):
    rows, depth = a_rows.shape
    return pl.pallas_call(
        functools.partial(rest_product_kernel, offsets, share),
        in_specs=[
            pl.BlockSpec(memory_space=pltpu.SMEM),
            pl.BlockSpec(memory_space=pltpu.VMEM),
            pl.BlockSpec(memory_space=pltpu.HBM),
        ]
        + [pl.BlockSpec(memory_space=pltpu.VMEM)] * len(parts),
        out_specs=pl.BlockSpec(memory_space=pltpu.VMEM),
        out_shape=jax.ShapeDtypeStruct((rows // 2, 2 * LANES), jnp.int32),
        scratch_shapes=[
            pltpu.VMEM((rows, depth), BF16),
            pltpu.VMEM((rows, LANES), jnp.int32),
            pltpu.VMEM((rows, rows), BF16),
            pltpu.VMEM((depth, 3 * LANES), BF16),
            pltpu.VMEM((rows, 4 * LANES), BF16),
            pltpu.SemaphoreType.DMA((rows // DEEP_BLOCK,)),
        ],
        compiler_params=params(32),
        cost_estimate=pl.CostEstimate(
            flops=2 * rows * (3 * depth + 4 * rows) * LANES, bytes_accessed=2 * rows * depth, transcendentals=0
        ),
        name="rest_products",
    )(my_index, order, in_hbm(a_rows), *parts)


def packed_terms(x, terms_ref, start):
    half = x.shape[0]
    first, second, third = (term.astype(F32) for term in split(x, 3))
    near = lane_ids(x.shape) < PANEL
    other = swap_halves(third)
    terms_ref[:half, start : start + LANES] = jnp.where(near, first, swap_halves(second)).astype(BF16)
    terms_ref[half:, start : start + LANES] = jnp.where(near, swap_halves(first), second).astype(BF16)
    terms_ref[:half, start + LANES : start + 2 * LANES] = jnp.where(near, third, other).astype(BF16)
    terms_ref[half:, start + LANES : start + 2 * LANES] = jnp.where(near, other, third).astype(BF16)


def leading_kernel(held, index_ref, arrived_ref, out_ref, terms_ref):
    packed_terms(arrived_ref[...], terms_ref, 0)
    width = -(-held // LANES) * LANES
    picks = one_hot(index_ref[:, :width], terms_ref.shape[0])
    got = whole_sum(jnp.dot(picks, terms_ref[...], preferred_element_type=F32))
    first, second = got[: held // 2], got[held // 2 : held]
    out_ref[0] = jnp.where(lane_ids(first.shape) < PANEL, first, second)


def leading_rows(index, arrived, held):
    rows = index.shape[1]
    return pl.pallas_call(
        functools.partial(leading_kernel, held),
        in_specs=[pl.BlockSpec(memory_space=pltpu.VMEM)] * 2,
        out_specs=pl.BlockSpec(memory_space=pltpu.VMEM),
        out_shape=jax.ShapeDtypeStruct((1, held // 2, LANES), F32),
        scratch_shapes=[pltpu.VMEM((rows, 2 * LANES), BF16)],
        compiler_params=params(),
        cost_estimate=pl.CostEstimate(
            flops=4 * held * rows * LANES, bytes_accessed=2 * rows * LANES, transcendentals=0
        ),
        name="leading_rows",
    )(index, arrived)


def eliminate(block, shift_row):
    rows = lax.broadcasted_iota(jnp.int32, (PANEL, PANEL), 0)
    columns = lax.broadcasted_iota(jnp.int32, (PANEL, PANEL), 1)
    flipped = jnp.transpose(block)
    mirrored = jnp.where(rows >= columns, block, flipped)
    diagonal = shift_row + jnp.sum(jnp.abs(mirrored), axis=0, keepdims=True)
    unit = (rows == columns).astype(F32)
    work = jnp.where(rows == columns, diagonal, mirrored)
    work = jnp.concatenate([work, unit], axis=1)
    height = 8
    groups = [work[start : start + height] for start in range(0, PANEL, height)]
    sublanes = lax.broadcasted_iota(jnp.int32, (height, LANES), 0)
    scaled_rows = []
    for k in range(PANEL):
        home, offset = divmod(k, height)
        row = groups[home][offset : offset + 1, :]
        row = row / row[:, k : k + 1]
        scaled_rows.append(row)
        for g in range(home, PANEL // height):
            column = jnp.broadcast_to(groups[g][:, k : k + 1], (height, LANES))
            if g == home:
                column = jnp.where(sublanes > offset, column, 0.0)
            groups[g] = groups[g] - column * row
    final = jnp.concatenate(groups, axis=0)
    scaled = jnp.concatenate(scaled_rows, axis=0)
    upper = jnp.where(columns >= rows, scaled[:, :PANEL], 0.0)
    pivots = jnp.sum(jnp.where(rows == columns, final[:, :PANEL], 0.0), axis=0, keepdims=True)
    return upper, final[:, PANEL:], pivots


def exact(lhs, rhs, dims):
    return lax.dot_general(lhs, rhs, (dims, ((), ())), precision=lax.Precision.HIGHEST, preferred_element_type=F32)


def update_kernel(offsets, blocks_held, columns, my_ref, index_ref, arrived_ref, shift_ref, resident_hbm, *refs):
    parts = refs[:-12]
    near_hbm, far_hbm, pivots_ref, leading_ref, tail_ref, resident_ref, terms_ref, lead_ref = refs[-12:-4]
    near_ref, far_ref, sem, sems = refs[-4:]
    fetch = pltpu.make_async_copy(resident_hbm, resident_ref, sem)
    fetch.start()
    my_index = my_ref[0]
    size = len(offsets)
    position = 0
    packed = blocks_held * PANEL // 2
    part_rows = PANEL // 2
    for part in parts:
        for number in range(part.shape[0]):
            owner = my_index ^ offsets[position]
            for start in range(0, blocks_held * PANEL, part_rows):
                held, inner = divmod(start, PANEL)
                if start < packed:
                    rows = part[number, start : start + part_rows, :PANEL]
                else:
                    rows = part[number, start - packed : start - packed + part_rows, PANEL:]
                target = pl.multiple_of((held * size + owner) * PANEL + inner, part_rows)
                leading_ref[pl.ds(target, part_rows), :] = rows
            position += 1
    upper, inverse, pivots = eliminate(leading_ref[:PANEL, :], shift_ref[...])
    pivots_ref[...] = pivots
    lower = jnp.transpose(upper)
    needed = tail_ref.shape[1]
    tail = exact(inverse, leading_ref[:needed, :], ((1,), (1,)))
    high, low = split(tail, 2)
    tail_ref[0:PANEL, :] = high
    tail_ref[PANEL : 2 * PANEL, :] = high
    tail_ref[2 * PANEL : 3 * PANEL, :] = low
    tail_ref[3 * PANEL :, :] = low

    block = A_BLOCK
    packed_terms(arrived_ref[...], terms_ref, 0)
    for start in range(0, lead_ref.shape[0], block):
        picks = one_hot(index_ref[:, start : start + block], lead_ref.shape[0])
        got = jnp.dot(picks, terms_ref[...], preferred_element_type=F32)
        lead_ref[start : start + block, :] = whole_sum(got)[:, :PANEL]
    fetch.wait()
    stores = []
    for number, start in enumerate(range(0, lead_ref.shape[0], block)):
        rows_here = slice(start, start + block)
        panel = exact(lead_ref[rows_here, :], inverse, ((1,), (1,))) / pivots
        shown = used = panel
        if start == 0:
            row_ids = lax.broadcasted_iota(jnp.int32, panel.shape, 0)
            top = jnp.logical_and(my_index == 0, row_ids < PANEL)
            used = jnp.where(top, 0.0, panel)
            filled = jnp.concatenate([lower, jnp.zeros((block - PANEL, PANEL), F32)], axis=0)
            shown = jnp.where(top, filled, panel)
        high, low = (term.astype(F32) for term in split(used, 2))
        pair = jnp.concatenate([high, low], axis=1).astype(BF16)
        factors = jnp.concatenate([pair, pair], axis=1)
        update = jnp.dot(factors, tail_ref[...], preferred_element_type=F32)
        shown = jnp.concatenate([shown, jnp.zeros_like(shown)], axis=1)
        near_ref[rows_here, :LANES] = jnp.where(lane_ids(shown.shape) < PANEL, shown, -update[:, :LANES])
        near_ref[rows_here, LANES:] = -update[:, LANES:columns]
        far_ref[rows_here, :] = (resident_ref[rows_here, :].astype(F32) - update[:, columns:]).astype(BF16)
        for which, (source, target) in enumerate(((near_ref, near_hbm), (far_ref, far_hbm))):
            store = pltpu.make_async_copy(
                source.at[pl.ds(start, block), :], target.at[pl.ds(start, block), :], sems.at[which, number]
            )
            store.start()
            stores.append(store)
    for store in stores:
        store.wait()


def updates(my_index, parts, offsets, index, arrived, shift, resident, blocks_held, columns):
    rows, width = resident.shape
    needed = columns + width
    held_rows = len(offsets) * blocks_held * PANEL
    vmem = pl.BlockSpec(memory_space=pltpu.VMEM)
    anywhere = pl.BlockSpec(memory_space=pltpu.HBM)
    return pl.pallas_call(
        functools.partial(update_kernel, offsets, blocks_held, columns),
        in_specs=[pl.BlockSpec(memory_space=pltpu.SMEM), vmem, vmem, vmem, anywhere] + [vmem] * len(parts),
        out_specs=[anywhere, anywhere, vmem],
        out_shape=[
            pltpu.HBM((rows, columns), F32),
            pltpu.HBM((rows, width), BF16),
            jax.ShapeDtypeStruct((1, PANEL), F32),
        ],
        scratch_shapes=[
            pltpu.VMEM((held_rows, PANEL), F32),
            pltpu.VMEM((4 * PANEL, needed), BF16),
            pltpu.VMEM((rows, width), BF16),
            pltpu.VMEM((rows, 2 * LANES), BF16),
            pltpu.VMEM((rows, PANEL), F32),
            pltpu.VMEM((rows, columns), F32),
            pltpu.VMEM((rows, width), BF16),
            pltpu.SemaphoreType.DMA,
            pltpu.SemaphoreType.DMA((2, rows // A_BLOCK)),
        ],
        compiler_params=params(32),
        cost_estimate=pl.CostEstimate(
            flops=2 * rows * needed * 4 * PANEL, bytes_accessed=4 * rows * (columns + width), transcendentals=0
        ),
        name="factor_and_update",
    )(my_index, index, arrived, shift, in_hbm(resident), *parts)


def formed_kernel(index_ref, arrived_ref, near_hbm, out_hbm, near_ref, terms_ref, out_ref, in_sems, out_sems):
    half = arrived_ref.shape[0]
    block = A_BLOCK
    starts = range(0, near_ref.shape[0], block)

    def rows_of(ref, start):
        return ref.at[pl.ds(start, block), :]

    fetches = [
        pltpu.make_async_copy(rows_of(near_hbm, start), rows_of(near_ref, start), in_sems.at[i])
        for i, start in enumerate(starts)
    ]
    for fetch in fetches:
        fetch.start()
    words = arrived_ref[:, LANES:]
    low_lanes = lane_ids(words.shape) < PANEL
    scale = jnp.exp2(((words & 255) - (BIAS + 15)).astype(F32)) * (1 / MARGIN)
    other = swap_halves(scale)
    first, second = (term.astype(F32) for term in split((words >> 16).astype(F32) * scale, 2))
    terms_ref[:half, 2 * LANES :] = jnp.where(low_lanes, first, swap_halves(second)).astype(BF16)
    terms_ref[half:, 2 * LANES :] = jnp.where(low_lanes, swap_halves(first), second).astype(BF16)
    words = arrived_ref[:, :LANES]
    low = (words >> 16).astype(F32) * jnp.where(low_lanes, scale, other)
    high = ((words << 16) >> 16).astype(F32) * jnp.where(low_lanes, other, scale)
    for side, values in enumerate((low, high)):
        first, second = split(values, 2)
        terms_ref[side * half : (side + 1) * half, :LANES] = first
        terms_ref[side * half : (side + 1) * half, LANES : 2 * LANES] = second

    stores = []
    for i, start in enumerate(starts):
        rows_here = slice(start, start + block)
        picks = one_hot(index_ref[:, rows_here], terms_ref.shape[0])
        got = jnp.dot(picks, terms_ref[...], preferred_element_type=F32)
        pair = got[:, 2 * LANES :]
        fetches[i].wait()
        held = near_ref[rows_here, :LANES]
        out_ref[rows_here, :LANES] = jnp.where(
            lane_ids(held.shape) < PANEL, held, (pair + swap_halves(pair)) + held
        )
        out_ref[rows_here, LANES:] = (got[:, :LANES] + got[:, LANES : 2 * LANES]) + near_ref[rows_here, LANES:]
        store = pltpu.make_async_copy(rows_of(out_ref, start), rows_of(out_hbm, start), out_sems.at[i])
        store.start()
        stores.append(store)
    for store in stores:
        store.wait()


def formed_columns(index, arrived, near):
    rows, columns = near.shape
    vmem = pl.BlockSpec(memory_space=pltpu.VMEM)
    anywhere = pl.BlockSpec(memory_space=pltpu.HBM)
    return pl.pallas_call(
        formed_kernel,
        in_specs=[vmem, vmem, anywhere],
        out_specs=anywhere,
        out_shape=pltpu.HBM((rows, columns), F32),
        input_output_aliases={2: 0},
        scratch_shapes=[
            pltpu.VMEM((rows, columns), F32),
            pltpu.VMEM((rows, 3 * LANES), BF16),
            pltpu.VMEM((rows, columns), F32),
            pltpu.SemaphoreType.DMA((rows // A_BLOCK,)),
            pltpu.SemaphoreType.DMA((rows // A_BLOCK,)),
        ],
        compiler_params=params(32),
        cost_estimate=pl.CostEstimate(
            flops=8 * rows * rows * LANES, bytes_accessed=8 * rows * columns, transcendentals=0
        ),
        name="formed_columns",
    )(index, arrived, near)


def swap_rows(x, group):
    rows, width = x.shape
    return lax.all_to_all(
        x.reshape(group, rows // group, width), "wide", split_axis=0, concat_axis=0, tiled=True
    ).reshape(rows, width)


def on_device(a_rows, xa_panel, za_panel, send_order, recv_order, shift, resident):
    rows = a_rows.shape[0]
    columns = xa_panel.shape[1]
    group = lax.axis_size("wide")
    my_index = lax.axis_index("wide").astype(jnp.int32).reshape(1)
    share = rows // group
    half = rows // 2
    few, apart = phases_of(group)

    order, packing = send_order, share
    if share % 16:
        order = send_order.reshape(group, 2, share // 2).transpose(1, 0, 2).reshape(1, rows)
        packing = 0
    source, slot = recv_order // share, recv_order % share
    index = (slot // (share // 2)) * half + source * (share // 2) + slot % (share // 2)

    lead_panel, rest_panel = split_panels(my_index, xa_panel, za_panel)
    send_picks, a_copy = order_picks(order, a_rows, packing)
    lead_parts = [lead_panel]
    for masks in few:
        lead_parts = exchange(join(lead_parts), masks, "wide")
    rest_parts = [rest_panel]
    for number, masks in enumerate(apart[:-2]):
        rest_parts = exchange(join(rest_parts), masks, "wide")
        if number == 0:
            lead_parts = tied(lead_parts, *rest_parts)

    lead_out = lead_products(my_index, a_copy, send_picks, lead_parts, offsets_of(few))
    lead_in = swap_rows(tied([lead_out], *rest_parts)[0], group)
    rest_parts = exchange(join(tied(rest_parts, lead_out)), apart[-2], "wide")
    other_parts = exchange(rest_parts[:1], apart[-1], "wide")[1:]

    needed = columns + resident.shape[1]
    blocks_held = -(-needed // (PANEL * group))
    leading_parts = [leading_rows(index, lead_in, blocks_held * PANEL)]
    for masks in few:
        leading_parts = exchange(join(leading_parts), masks, "wide")
        if masks is few[0]:
            later_parts = exchange(tied(rest_parts[1:], *leading_parts), apart[-1], "wide")
    late = len(later_parts) // 2
    rest_parts = rest_parts + other_parts + later_parts[late:]
    rest_out = rest_products(my_index, order, a_rows, rest_parts, offsets_of(apart), packing)
    rest_in = swap_rows(tied([rest_out], *leading_parts)[0], group)
    near, updated, pivots = updates(
        my_index,
        leading_parts,
        offsets_of(few),
        index,
        tied([lead_in], rest_out)[0],
        shift[None, :],
        resident,
        blocks_held,
        columns,
    )
    factored = formed_columns(index, rest_in, near)
    return (factored, updated, pivots[0])


def solution(mesh):
    placed = (
        P(("parts", "wide"), None),
        P(("parts", "wide"), None),
        P(("parts", "wide"), None),
        P(("parts", "wide"), None),
        P(("parts", "wide"), None),
        P("parts"),
        P(("parts", "wide"), None),
    )
    return jax.shard_map(
        on_device,
        mesh=mesh,
        in_specs=placed,
        out_specs=(P(("parts", "wide"), None), P(("parts", "wide"), None), P("parts")),
        check_vma=False,
    )
```

profile of v0, /device:TPU:0, one launch (start us, length us, event | category | flops | bytes accessed | tf_op | source)
XLA Modules:
  0.0 81.4 jit_solution(13722162143872600123)
XLA Ops:
  0.6 1.0 %split_panels.1 = (bf16[1,128,128]{2,1,0:T(8,128)(2,1)S(1)}, bf16[1,128,384]{2,1,0:T(8,128)(2,1)S(1)}) custom-call(s32[1]{0:T(128)} %bitcast.my_ref, bf16[128,256]{1,0:T(8,128)(2,1)} %xa_hbm.1, bf16[128,256]{1,0:T(8,128)(2,1)} %za_hbm.1), custom_call_target="tpu_custom_call" | custom-call | tf_op jit(solution)/shard_map/split_panels/pallas_call | solution.py:167
  1.6 4.1 %collective-permute-start.2 = (bf16[1,128,128]{2,1,0:T(8,128)(2,1)S(1)}, bf16[1,128,128]{2,1,0:T(8,128)(2,1)S(1)}, u32[]{:S(2)}, u32[]{:S(2)}) collective-permute-start(bf16[1,128,128]{2,1,0:T(8,128)(2,1)S(1)} %get-tuple-element.23), channel_id=1, source_target_pairs={{0,8},{1,9},{2,10},{3,11},{4,12},{5,13},{6,14},{7,15},{8,0},{9,1},... | collective-permute-start | bytes 98312 | tf_op jit(solution)/shard_map/ppermute | solution.py:94
  5.7 1.6 %collective-permute-start.3 = (bf16[1,128,128]{2,1,0:T(8,128)(2,1)S(1)}, bf16[1,128,128]{2,1,0:T(8,128)(2,1)S(1)}, u32[]{:S(2)}, u32[]{:S(2)}) collective-permute-start(bf16[1,128,128]{2,1,0:T(8,128)(2,1)S(1)} %get-tuple-element.23), channel_id=1, source_target_pairs={{0,4},{1,5},{2,6},{3,7},{4,0},{5,1},{6,2},{7,3},{8,12},{9,13},{10,... | collective-permute-start | bytes 98312 | tf_op jit(solution)/shard_map/ppermute | solution.py:94
  7.3 1.9 %collective-permute-start = (bf16[1,128,384]{2,1,0:T(8,128)(2,1)S(1)}, bf16[1,128,384]{2,1,0:T(8,128)(2,1)S(1)}, u32[]{:S(2)}, u32[]{:S(2)}) collective-permute-start(bf16[1,128,384]{2,1,0:T(8,128)(2,1)S(1)} %get-tuple-element.20), channel_id=1, source_target_pairs={{0,8},{1,9},{2,10},{3,11},{4,12},{5,13},{6,14},{7,15},{8,0},{9,1},... | collective-permute-start | bytes 294920 | tf_op jit(solution)/shard_map/ppermute | solution.py:94
  9.3 0.4 collective-permute-done.3
  9.7 3.4 %collective-permute-done.4 = bf16[1,128,128]{2,1,0:T(8,128)(2,1)S(1)} collective-permute-done((bf16[1,128,128]{2,1,0:T(8,128)(2,1)S(1)}, bf16[1,128,128]{2,1,0:T(8,128)(2,1)S(1)}, u32[]{:S(2)}, u32[]{:S(2)}) %collective-permute-start.4) | collective-permute-done | bytes 32800 | tf_op jit(solution)/shard_map/ppermute | solution.py:94
  13.0 1.5 %collective-permute-start.5 = (bf16[4,128,128]{2,1,0:T(8,128)(2,1)S(1)}, bf16[4,128,128]{2,1,0:T(8,128)(2,1)S(1)}, u32[]{:S(2)}, u32[]{:S(2)}) collective-permute-start(bf16[4,128,128]{2,1,0:T(8,128)(2,1)S(1)} %constant_dynamic-update-slice_fusion.2.refs_0_), channel_id=1, source_target_pairs={{0,2},{1,3},{2,0},{3,1},{4,6},{5,7},{6,4},{7,5},{8,10},{9,11},{10,... | collective-permute-start | bytes 393224 | tf_op jit(solution)/shard_map/ppermute | solution.py:94
  14.6 0.6 collective-permute-start.7
  15.2 0.2 collective-permute-done
  15.4 1.7 %collective-permute-start.1 = (bf16[2,128,384]{2,1,0:T(8,128)(2,1)S(1)}, bf16[2,128,384]{2,1,0:T(8,128)(2,1)S(1)}, u32[]{:S(2)}, u32[]{:S(2)}) collective-permute-start(bf16[2,128,384]{2,1,0:T(8,128)(2,1)S(1)} %constant_dynamic-update-slice_fusion), channel_id=1, source_target_pairs={{0,4},{1,5},{2,6},{3,7},{4,0},{5,1},{6,2},{7,3},{8,12},{9,13},{10,... | collective-permute-start | bytes 589832 | tf_op jit(solution)/shard_map/ppermute | solution.py:94
  17.0 2.5 %order_picks.1 = (bf16[1280,1280]{1,0:T(8,128)(2,1)S(1)}, bf16[1280,2048]{1,0:T(8,128)(2,1)S(1)}) custom-call(s32[1,1280]{1,0:T(1,128)} %order_ref.1, bf16[1280,2048]{1,0:T(8,128)(2,1)} %a_hbm.3), custom_call_target="tpu_custom_call" | custom-call | flops 6553600 | bytes 10485760 | tf_op jit(solution)/shard_map/order_picks/pallas_call | solution.py:134
  19.6 0.8 collective-permute-done.7.refs_3_
  20.3 3.2 %lead_products.1 = f32[640,128]{1,0:T(8,128)} custom-call(s32[1]{0:T(128)} %bitcast.my_ref, bf16[1280,2048]{1,0:T(8,128)(2,1)S(1)} %get-tuple-element.21.a_ref, bf16[1280,1280]{1,0:T(8,128)(2,1)S(1)} %get-tuple-element.22.picks_ref, bf16[4,128,128]{2,1,0:T(8,128)(2,1)S(1)} %constant_dynamic-update-slice_fusion.2.refs_0_, ...), custom_call_target="tpu_custom_call" | custom-call | flops 1509949440 | bytes 5242880 | tf_op jit(solution)/shard_map/lead_products/pallas_call | solution.py:220
  23.6 4.2 %all-to-all-start = ((f32[16,40,128]{2,1,0:T(8,128)}), f32[16,40,128]{2,1,0:T(8,128)S(1)}, u32[]{:S(2)}, u32[]{:S(2)}) async-start(f32[16,40,128]{2,1,0:T(8,128)} %bitcast.1), calls=%async_computation | async-start | bytes 655360 | tf_op jit(solution)/shard_map/all_to_all | solution.py:580
  27.9 2.0 %collective-permute-start.8 = (bf16[4,128,384]{2,1,0:T(8,128)(2,1)S(1)}, bf16[4,128,384]{2,1,0:T(8,128)(2,1)S(1)}, u32[]{:S(2)}, u32[]{:S(2)}) collective-permute-start(bf16[4,128,384]{2,1,0:T(8,128)(2,1)S(1)} %constant_dynamic-update-slice_fusion.6.refs_0_), channel_id=1, source_target_pairs={{0,2},{1,3},{2,0},{3,1},{4,6},{5,7},{6,4},{7,5},{8,10},{9,11},{10,... | collective-permute-start | bytes 1179656 | tf_op jit(solution)/shard_map/ppermute | solution.py:94
  29.9 0.1 fusion.index_ref
  30.0 9.0 %all-to-all-done = f32[16,40,128]{2,1,0:T(8,128)S(1)} async-done(((f32[16,40,128]{2,1,0:T(8,128)}), f32[16,40,128]{2,1,0:T(8,128)S(1)}, u32[]{:S(2)}, u32[]{:S(2)}) %all-to-all-start) | async-done | bytes 327712 | tf_op jit(solution)/shard_map/all_to_all | solution.py:580
  38.9 0.5 leading_rows.1
  39.5 1.6 %collective-permute-start.10 = (f32[1,64,128]{2,1,0:T(8,128)S(1)}, f32[1,64,128]{2,1,0:T(8,128)S(1)}, u32[]{:S(2)}, u32[]{:S(2)}) collective-permute-start(f32[1,64,128]{2,1,0:T(8,128)S(1)} %leading_rows.1), channel_id=1, source_target_pairs={{0,8},{1,9},{2,10},{3,11},{4,12},{5,13},{6,14},{7,15},{8,0},{9,1},... | collective-permute-start | bytes 98312 | tf_op jit(solution)/shard_map/ppermute | solution.py:94
  41.0 0.2 collective-permute-start.11
  41.2 2.7 %collective-permute-start.12 = (f32[1,64,128]{2,1,0:T(8,128)S(1)}, f32[1,64,128]{2,1,0:T(8,128)S(1)}, u32[]{:S(2)}, u32[]{:S(2)}) collective-permute-start(f32[1,64,128]{2,1,0:T(8,128)S(1)} %leading_rows.1), channel_id=1, source_target_pairs={{0,12},{1,13},{2,14},{3,15},{4,8},{5,9},{6,10},{7,11},{8,4},{9,5},... | collective-permute-start | bytes 98312 | tf_op jit(solution)/shard_map/ppermute | solution.py:94
  44.0 1.0 %collective-permute-done.10 = f32[1,64,128]{2,1,0:T(8,128)S(1)} collective-permute-done((f32[1,64,128]{2,1,0:T(8,128)S(1)}, f32[1,64,128]{2,1,0:T(8,128)S(1)}, u32[]{:S(2)}, u32[]{:S(2)}) %collective-permute-start.10) | collective-permute-done | bytes 32800 | tf_op jit(solution)/shard_map/ppermute | solution.py:94
  45.0 0.2 collective-permute-done.11
  45.1 1.8 %collective-permute-done.12 = f32[1,64,128]{2,1,0:T(8,128)S(1)} collective-permute-done((f32[1,64,128]{2,1,0:T(8,128)S(1)}, f32[1,64,128]{2,1,0:T(8,128)S(1)}, u32[]{:S(2)}, u32[]{:S(2)}) %collective-permute-start.12) | collective-permute-done | bytes 32800 | tf_op jit(solution)/shard_map/ppermute | solution.py:94
  47.0 1.4 %collective-permute-start.14 = (f32[4,64,128]{2,1,0:T(8,128)S(1)}, f32[4,64,128]{2,1,0:T(8,128)S(1)}, u32[]{:S(2)}, u32[]{:S(2)}) collective-permute-start(f32[4,64,128]{2,1,0:T(8,128)S(1)} %pad_maximum_fusion.refs_0_), channel_id=1, source_target_pairs={{0,2},{1,3},{2,0},{3,1},{4,6},{5,7},{6,4},{7,5},{8,10},{9,11},{10,... | collective-permute-start | bytes 393224 | tf_op jit(solution)/shard_map/ppermute | solution.py:94
  48.3 0.2 collective-permute-start.15
  48.6 0.6 collective-permute-start.16
  49.2 7.6 %rest_products.1 = s32[640,256]{1,0:T(8,128)} custom-call(s32[1]{0:T(128)} %bitcast.my_ref, s32[1,1280]{1,0:T(1,128)S(1)} %copy-done, bf16[1280,2048]{1,0:T(8,128)(2,1)} %a_hbm.3, bf16[4,128,384]{2,1,0:T(8,128)(2,1)S(1)} %constant_dynamic-update-slice_fusion.6.refs_0_, bf16[4,128,384]{2,1,0:T(8,128)(2,1)S(1)} %collective-permute-done.8.refs_1_, ...), custom_call_target="tpu_custom_call" | custom-call | flops 3690987520 | bytes 5242880 | tf_op jit(solution)/shard_map/rest_products/pallas_call | solution.py:305
  56.8 4.1 %all-to-all-start.1 = ((s32[16,40,256]{2,1,0:T(8,128)}), s32[16,40,256]{2,1,0:T(8,128)S(1)}, u32[]{:S(2)}, u32[]{:S(2)}) async-start(s32[16,40,256]{2,1,0:T(8,128)} %bitcast.3), calls=%async_computation.1 | async-start | bytes 1310720 | tf_op jit(solution)/shard_map/all_to_all | solution.py:580
  60.9 12.0 %factor_and_update.1 = (f32[1280,256]{1,0:T(8,128)}, bf16[1280,1024]{1,0:T(8,128)(2,1)}, f32[1,64]{1,0:T(1,128)}) custom-call(s32[1]{0:T(128)} %bitcast.my_ref, s32[1,1280]{1,0:T(1,128)S(1)} %fusion.index_ref, f32[640,128]{1,0:T(8,128)S(1)} %bitcast.8, f32[1,64]{1,0:T(1,128)S(1)} %bitcast.10, bf16[1280,1024]{1,0:T(8,128)(2,1)} %resident_hbm.1, ...), custom_call_target="tpu_custom_call" | custom-call | flops 838860800 | bytes 6553600 | tf_op jit(solution)/shard_map/factor_and_update/pallas_call | solution.py:477
  72.9 4.6 %all-to-all-done.1 = s32[16,40,256]{2,1,0:T(8,128)S(1)} async-done(((s32[16,40,256]{2,1,0:T(8,128)}), s32[16,40,256]{2,1,0:T(8,128)S(1)}, u32[]{:S(2)}, u32[]{:S(2)}) %all-to-all-start.1) | async-done | bytes 655392 | tf_op jit(solution)/shard_map/all_to_all | solution.py:580
  77.5 3.8 %formed_columns.1 = f32[1280,256]{1,0:T(8,128)} custom-call(s32[1,1280]{1,0:T(1,128)S(1)} %fusion.index_ref, s32[640,256]{1,0:T(8,128)S(1)} %bitcast.9, f32[1280,256]{1,0:T(8,128)} %get-tuple-element.34.near_hbm), custom_call_target="tpu_custom_call", output_to_operand_aliasing={{}: (2, {})} | custom-call | flops 1677721600 | bytes 2621440 | tf_op jit(solution)/shard_map/formed_columns/pallas_call | solution.py:557
  (29 shorter events, 0.2 us)
Async XLA Ops:
  1.6 7.6 %collective-permute-start.2 = (bf16[1,128,128]{2,1,0:T(8,128)(2,1)S(1)}, bf16[1,128,128]{2,1,0:T(8,128)(2,1)S(1)}, u32[]{:S(2)}, u32[]{:S(2)}) collective-permute-start(bf16[1,128,128]{2,1,0:T(8,128)(2,1)S(1)} %get-tuple-element.23), channel_id=1, source_target_pairs={{0,8},{1,9},{2,10},{3,11},{4,12},{5,13},{6,14},{7,15},{8,0},{9,1},... | collective-permute-start | bytes 98312 | tf_op jit(solution)/shard_map/ppermute | solution.py:94
  5.7 3.9 %collective-permute-start.3 = (bf16[1,128,128]{2,1,0:T(8,128)(2,1)S(1)}, bf16[1,128,128]{2,1,0:T(8,128)(2,1)S(1)}, u32[]{:S(2)}, u32[]{:S(2)}) collective-permute-start(bf16[1,128,128]{2,1,0:T(8,128)(2,1)S(1)} %get-tuple-element.23), channel_id=1, source_target_pairs={{0,4},{1,5},{2,6},{3,7},{4,0},{5,1},{6,2},{7,3},{8,12},{9,13},{10,... | collective-permute-start | bytes 98312 | tf_op jit(solution)/shard_map/ppermute | solution.py:94
  7.3 5.7 %collective-permute-start.4 = (bf16[1,128,128]{2,1,0:T(8,128)(2,1)S(1)}, bf16[1,128,128]{2,1,0:T(8,128)(2,1)S(1)}, u32[]{:S(2)}, u32[]{:S(2)}) collective-permute-start(bf16[1,128,128]{2,1,0:T(8,128)(2,1)S(1)} %get-tuple-element.23), channel_id=1, source_target_pairs={{0,12},{1,13},{2,14},{3,15},{4,8},{5,9},{6,10},{7,11},{8,4},{9,5},... | collective-permute-start | bytes 98312 | tf_op jit(solution)/shard_map/ppermute | solution.py:94
  7.3 8.0 %collective-permute-start = (bf16[1,128,384]{2,1,0:T(8,128)(2,1)S(1)}, bf16[1,128,384]{2,1,0:T(8,128)(2,1)S(1)}, u32[]{:S(2)}, u32[]{:S(2)}) collective-permute-start(bf16[1,128,384]{2,1,0:T(8,128)(2,1)S(1)} %get-tuple-element.20), channel_id=1, source_target_pairs={{0,8},{1,9},{2,10},{3,11},{4,12},{5,13},{6,14},{7,15},{8,0},{9,1},... | collective-permute-start | bytes 294920 | tf_op jit(solution)/shard_map/ppermute | solution.py:94
  13.0 6.5 %collective-permute-start.5 = (bf16[4,128,128]{2,1,0:T(8,128)(2,1)S(1)}, bf16[4,128,128]{2,1,0:T(8,128)(2,1)S(1)}, u32[]{:S(2)}, u32[]{:S(2)}) collective-permute-start(bf16[4,128,128]{2,1,0:T(8,128)(2,1)S(1)} %constant_dynamic-update-slice_fusion.2.refs_0_), channel_id=1, source_target_pairs={{0,2},{1,3},{2,0},{3,1},{4,6},{5,7},{6,4},{7,5},{8,10},{9,11},{10,... | collective-permute-start | bytes 393224 | tf_op jit(solution)/shard_map/ppermute | solution.py:94
  14.6 5.0 %collective-permute-start.6 = (bf16[4,128,128]{2,1,0:T(8,128)(2,1)S(1)}, bf16[4,128,128]{2,1,0:T(8,128)(2,1)S(1)}, u32[]{:S(2)}, u32[]{:S(2)}) collective-permute-start(bf16[4,128,128]{2,1,0:T(8,128)(2,1)S(1)} %constant_dynamic-update-slice_fusion.2.refs_0_), channel_id=1, source_target_pairs={{0,1},{1,0},{2,3},{3,2},{4,5},{5,4},{6,7},{7,6},{8,9},{9,8},{10,11... | collective-permute-start | bytes 393224 | tf_op jit(solution)/shard_map/ppermute | solution.py:94
  14.6 5.8 %collective-permute-start.7 = (bf16[4,128,128]{2,1,0:T(8,128)(2,1)S(1)}, bf16[4,128,128]{2,1,0:T(8,128)(2,1)S(1)}, u32[]{:S(2)}, u32[]{:S(2)}) collective-permute-start(bf16[4,128,128]{2,1,0:T(8,128)(2,1)S(1)} %constant_dynamic-update-slice_fusion.2.refs_0_), channel_id=1, source_target_pairs={{0,3},{1,2},{2,1},{3,0},{4,7},{5,6},{6,5},{7,4},{8,11},{9,10},{10,... | collective-permute-start | bytes 393224 | tf_op jit(solution)/shard_map/ppermute | solution.py:94
  15.4 8.2 %collective-permute-start.1 = (bf16[2,128,384]{2,1,0:T(8,128)(2,1)S(1)}, bf16[2,128,384]{2,1,0:T(8,128)(2,1)S(1)}, u32[]{:S(2)}, u32[]{:S(2)}) collective-permute-start(bf16[2,128,384]{2,1,0:T(8,128)(2,1)S(1)} %constant_dynamic-update-slice_fusion), channel_id=1, source_target_pairs={{0,4},{1,5},{2,6},{3,7},{4,0},{5,1},{6,2},{7,3},{8,12},{9,13},{10,... | collective-permute-start | bytes 589832 | tf_op jit(solution)/shard_map/ppermute | solution.py:94
  20.3 9.5 %copy-start.2 = (s32[1,1280]{1,0:T(1,128)S(1)}, s32[1,1280]{1,0:T(1,128)}, u32[]{:S(2)}) copy-start(s32[1,1280]{1,0:T(1,128)} %param.11) | copy-start | bytes 15364
  20.3 28.8 %copy-start = (s32[1,1280]{1,0:T(1,128)S(1)}, s32[1,1280]{1,0:T(1,128)}, u32[]{:S(2)}) copy-start(s32[1,1280]{1,0:T(1,128)} %order_ref.1) | copy-start | bytes 15364
  23.6 15.4 %all-to-all-start = ((f32[16,40,128]{2,1,0:T(8,128)}), f32[16,40,128]{2,1,0:T(8,128)S(1)}, u32[]{:S(2)}, u32[]{:S(2)}) async-start(f32[16,40,128]{2,1,0:T(8,128)} %bitcast.1), calls=%async_computation | async-start | bytes 655360 | tf_op jit(solution)/shard_map/all_to_all | solution.py:580
  27.9 16.1 %collective-permute-start.8 = (bf16[4,128,384]{2,1,0:T(8,128)(2,1)S(1)}, bf16[4,128,384]{2,1,0:T(8,128)(2,1)S(1)}, u32[]{:S(2)}, u32[]{:S(2)}) collective-permute-start(bf16[4,128,384]{2,1,0:T(8,128)(2,1)S(1)} %constant_dynamic-update-slice_fusion.6.refs_0_), channel_id=1, source_target_pairs={{0,2},{1,3},{2,0},{3,1},{4,6},{5,7},{6,4},{7,5},{8,10},{9,11},{10,... | collective-permute-start | bytes 1179656 | tf_op jit(solution)/shard_map/ppermute | solution.py:94
  39.5 5.5 %collective-permute-start.10 = (f32[1,64,128]{2,1,0:T(8,128)S(1)}, f32[1,64,128]{2,1,0:T(8,128)S(1)}, u32[]{:S(2)}, u32[]{:S(2)}) collective-permute-start(f32[1,64,128]{2,1,0:T(8,128)S(1)} %leading_rows.1), channel_id=1, source_target_pairs={{0,8},{1,9},{2,10},{3,11},{4,12},{5,13},{6,14},{7,15},{8,0},{9,1},... | collective-permute-start | bytes 98312 | tf_op jit(solution)/shard_map/ppermute | solution.py:94
  41.0 4.1 %collective-permute-start.11 = (f32[1,64,128]{2,1,0:T(8,128)S(1)}, f32[1,64,128]{2,1,0:T(8,128)S(1)}, u32[]{:S(2)}, u32[]{:S(2)}) collective-permute-start(f32[1,64,128]{2,1,0:T(8,128)S(1)} %leading_rows.1), channel_id=1, source_target_pairs={{0,4},{1,5},{2,6},{3,7},{4,0},{5,1},{6,2},{7,3},{8,12},{9,13},{10,... | collective-permute-start | bytes 98312 | tf_op jit(solution)/shard_map/ppermute | solution.py:94
  41.2 5.7 %collective-permute-start.12 = (f32[1,64,128]{2,1,0:T(8,128)S(1)}, f32[1,64,128]{2,1,0:T(8,128)S(1)}, u32[]{:S(2)}, u32[]{:S(2)}) collective-permute-start(f32[1,64,128]{2,1,0:T(8,128)S(1)} %leading_rows.1), channel_id=1, source_target_pairs={{0,12},{1,13},{2,14},{3,15},{4,8},{5,9},{6,10},{7,11},{8,4},{9,5},... | collective-permute-start | bytes 98312 | tf_op jit(solution)/shard_map/ppermute | solution.py:94
  43.9 5.2 %collective-permute-start.9 = (bf16[4,128,384]{2,1,0:T(8,128)(2,1)S(1)}, bf16[4,128,384]{2,1,0:T(8,128)(2,1)S(1)}, u32[]{:S(2)}, u32[]{:S(2)}) collective-permute-start(bf16[4,128,384]{2,1,0:T(8,128)(2,1)S(1)} %constant_dynamic-update-slice_fusion.6.refs_0_), channel_id=1, source_target_pairs={{0,1},{1,0},{2,3},{3,2},{4,5},{5,4},{6,7},{7,6},{8,9},{9,8},{10,11... | collective-permute-start | bytes 1179656 | tf_op jit(solution)/shard_map/ppermute | solution.py:94
  46.9 2.2 %collective-permute-start.13 = (bf16[4,128,384]{2,1,0:T(8,128)(2,1)S(1)}, bf16[4,128,384]{2,1,0:T(8,128)(2,1)S(1)}, u32[]{:S(2)}, u32[]{:S(2)}) collective-permute-start(bf16[4,128,384]{2,1,0:T(8,128)(2,1)S(1)} %collective-permute-done.8.refs_1_), channel_id=1, source_target_pairs={{0,1},{1,0},{2,3},{3,2},{4,5},{5,4},{6,7},{7,6},{8,9},{9,8},{10,11... | collective-permute-start | bytes 1179656 | tf_op jit(solution)/shard_map/ppermute | solution.py:94
  46.9 14.0 %copy-start.1 = (f32[64]{0:T(128)S(1)}, f32[64]{0:T(128)}, u32[]{:S(2)}) copy-start(f32[64]{0:T(128)} %param.12) | copy-start | bytes 772
  47.0 9.8 %collective-permute-start.14 = (f32[4,64,128]{2,1,0:T(8,128)S(1)}, f32[4,64,128]{2,1,0:T(8,128)S(1)}, u32[]{:S(2)}, u32[]{:S(2)}) collective-permute-start(f32[4,64,128]{2,1,0:T(8,128)S(1)} %pad_maximum_fusion.refs_0_), channel_id=1, source_target_pairs={{0,2},{1,3},{2,0},{3,1},{4,6},{5,7},{6,4},{7,5},{8,10},{9,11},{10,... | collective-permute-start | bytes 393224 | tf_op jit(solution)/shard_map/ppermute | solution.py:94
  48.3 8.4 %collective-permute-start.15 = (f32[4,64,128]{2,1,0:T(8,128)S(1)}, f32[4,64,128]{2,1,0:T(8,128)S(1)}, u32[]{:S(2)}, u32[]{:S(2)}) collective-permute-start(f32[4,64,128]{2,1,0:T(8,128)S(1)} %pad_maximum_fusion.refs_0_), channel_id=1, source_target_pairs={{0,1},{1,0},{2,3},{3,2},{4,5},{5,4},{6,7},{7,6},{8,9},{9,8},{10,11... | collective-permute-start | bytes 393224 | tf_op jit(solution)/shard_map/ppermute | solution.py:94
  48.6 8.2 %collective-permute-start.16 = (f32[4,64,128]{2,1,0:T(8,128)S(1)}, f32[4,64,128]{2,1,0:T(8,128)S(1)}, u32[]{:S(2)}, u32[]{:S(2)}) collective-permute-start(f32[4,64,128]{2,1,0:T(8,128)S(1)} %pad_maximum_fusion.refs_0_), channel_id=1, source_target_pairs={{0,3},{1,2},{2,1},{3,0},{4,7},{5,6},{6,5},{7,4},{8,11},{9,10},{10,... | collective-permute-start | bytes 393224 | tf_op jit(solution)/shard_map/ppermute | solution.py:94
  56.8 20.7 %all-to-all-start.1 = ((s32[16,40,256]{2,1,0:T(8,128)}), s32[16,40,256]{2,1,0:T(8,128)S(1)}, u32[]{:S(2)}, u32[]{:S(2)}) async-start(s32[16,40,256]{2,1,0:T(8,128)} %bitcast.3), calls=%async_computation.1 | async-start | bytes 1310720 | tf_op jit(solution)/shard_map/all_to_all | solution.py:580
where the time goes:
time: 81.9 us; the launch traced here: 81.4 us
  Pallas kernels  30.6 us (37%)
  starting transfers between devices  28.4 us (35%)
  waiting for transfers between devices  21.3 us (26%)
  between operations  0.97 us (1%)
    ppermute x17, starting transfers between devices, exchange(): lax.ppermute(part, axis, [(i, i ^ mask) for i in range(size)])  20 us
    all_to_all x2, waiting for transfers between devices, swap_rows(): lax.all_to_all(x.reshape(group, rows // group, width), 'wide', split_axis...  13.6 us
    pallas_call x1, Pallas kernels, updates(): pl.pallas_call(functools.partial(update_kernel, offsets, blocks_held, col...  12 us
    all_to_all x2, starting transfers between devices, swap_rows(): lax.all_to_all(x.reshape(group, rows // group, width), 'wide', split_axis...  8.36 us
    ppermute x17, waiting for transfers between devices, exchange(): lax.ppermute(part, axis, [(i, i ^ mask) for i in range(size)])  7.68 us
    pallas_call x1, Pallas kernels, rest_products(): pl.pallas_call(functools.partial(rest_product_kernel, offsets, share), in...  7.56 us
    pallas_call x1, Pallas kernels, formed_columns(): pl.pallas_call(formed_kernel, in_specs=[vmem, vmem, anywhere], out_specs=...  3.78 us
    pallas_call x1, Pallas kernels, lead_products(): pl.pallas_call(functools.partial(lead_product_kernel, offsets), in_specs=...  3.23 us
  transfers between devices with their start and end apart: 19, of which 9 were waited for; matrix products, arithmetic and copies ran while one was open for 0% of the time, Pallas kernels for 32%

commit v1 on v0

--- a/solution.py
+++ b/solution.py
@@ -223,7 +223,7 @@
         out_specs=pl.BlockSpec(memory_space=pltpu.VMEM),
         out_shape=jax.ShapeDtypeStruct((rows // 2, LANES), F32),
         scratch_shapes=[pltpu.VMEM((depth, LANES), BF16), pltpu.VMEM((rows, 2 * LANES), BF16)],
-        compiler_params=params(),
+        compiler_params=params(24),
         cost_estimate=pl.CostEstimate(
             flops=2 * rows * (depth + 2 * rows) * LANES, bytes_accessed=2 * rows * depth, transcendentals=0
         ),
@@ -236,11 +236,21 @@
 ROUNDER = 1.5 * 2.0**23
 
 
+def tight_split(part):
+    first = -(-part // 16) * 8
+    return first if part % 8 == 0 and part <= PANEL and 2 * first - part >= 8 else 0
+
+
+def words_shape(half, part):
+    first = tight_split(part)
+    return (half // part * (part + first), LANES) if first else (half, 2 * LANES)
+
+
 def nearest(x):
     return (x + ROUNDER) - ROUNDER
 
 
-def rest_product_kernel(offsets, share, my_ref, order_ref, a_hbm, *refs):
+def rest_product_kernel(offsets, share, part_rows, my_ref, order_ref, a_hbm, *refs):
     parts, (out_ref, a_ref, at_ref, picks_ref, panel_ref, terms_ref, sems) = refs[:-7], refs[-7:]
     rows = a_ref.shape[0]
     half = rows // 2
@@ -289,21 +299,49 @@
         far = got[:, :LANES] * 256.0 + got[:, LANES : 2 * LANES]
         pair = got[:, 2 * LANES : 3 * LANES]
         pair = jnp.where(lane_ids(pair.shape) < PANEL, pair * 256.0, pair)
-        near = (pair + swap_halves(pair)).astype(jnp.int32) * 65536 + (got[:, 3 * LANES :].astype(jnp.int32) + BIAS)
-        return far.astype(jnp.int32), near
+        near = (pair + swap_halves(pair)).astype(jnp.int32)
+        return far.astype(jnp.int32), near, got[:, 3 * LANES :]
 
     block = half // 2
+    first = tight_split(part_rows)
+    low_lanes = lane_ids((8, LANES)) < PANEL
+    eights = lax.broadcasted_iota(jnp.int32, (8, LANES), 0)
+    places = lax.broadcasted_iota(jnp.int32, (part_rows, LANES), 0) + PANEL
     for start in range(0, half, block):
-        far_low, near_low = coded(start, block)
-        far_high, near_high = coded(half + start, block)
-        out_ref[start : start + block, :LANES] = far_low * 65536 + (far_high & 65535)
-        out_ref[start : start + block, LANES:] = jnp.where(lane_ids(near_low.shape) < PANEL, near_low, near_high)
-
-
-def rest_products(my_index, order, a_rows, parts, offsets, share):
+        far_low, near_low, exponent_low = coded(start, block)
+        far_high, near_high, exponent_high = coded(half + start, block)
+        far = far_low * 65536 + (far_high & 65535)
+        if not first:
+            near = jnp.where(
+                lane_ids(near_low.shape) < PANEL,
+                near_low * 65536 + (exponent_low.astype(jnp.int32) + BIAS),
+                near_high * 65536 + (exponent_high.astype(jnp.int32) + BIAS),
+            )
+            out_ref[start : start + block, :LANES] = far
+            out_ref[start : start + block, LANES:] = near
+            continue
+        near = near_low * 65536 + (near_high & 65535)
+        second = part_rows - first
+        mine = lane_ids((part_rows, LANES)) == places
+        for inner in range(0, block, part_rows):
+            base = (start + inner) // part_rows * (part_rows + first)
+            words = near[inner : inner + part_rows]
+            rows = [
+                jnp.sum(jnp.where(mine, exponent[inner : inner + part_rows], 0.0), axis=0, keepdims=True)
+                for exponent in (exponent_low, exponent_high)
+            ]
+            rows = jnp.where(eights == 0, rows[0], jnp.where(eights == 1, rows[1], 0.0)).astype(jnp.int32)
+            out_ref[base : base + part_rows, :] = far[inner : inner + part_rows]
+            base += part_rows
+            spare = [words[: first - second - 8]] if first > second + 8 else []
+            both = jnp.concatenate([words[first:], rows, *spare], axis=0)
+            out_ref[base : base + first, :] = jnp.where(lane_ids(both.shape) < PANEL, words[:first], both)
+
+
+def rest_products(my_index, order, a_rows, parts, offsets, share, part_rows):
     rows, depth = a_rows.shape
     return pl.pallas_call(
-        functools.partial(rest_product_kernel, offsets, share),
+        functools.partial(rest_product_kernel, offsets, share, part_rows),
         in_specs=[
             pl.BlockSpec(memory_space=pltpu.SMEM),
             pl.BlockSpec(memory_space=pltpu.VMEM),
@@ -311,7 +349,7 @@
         ]
         + [pl.BlockSpec(memory_space=pltpu.VMEM)] * len(parts),
         out_specs=pl.BlockSpec(memory_space=pltpu.VMEM),
-        out_shape=jax.ShapeDtypeStruct((rows // 2, 2 * LANES), jnp.int32),
+        out_shape=jax.ShapeDtypeStruct(words_shape(rows // 2, part_rows), jnp.int32),
         scratch_shapes=[
             pltpu.VMEM((rows, depth), BF16),
             pltpu.VMEM((rows, LANES), jnp.int32),
@@ -502,8 +540,56 @@
     )(my_index, index, arrived, shift, in_hbm(resident), *parts)
 
 
-def formed_kernel(index_ref, arrived_ref, near_hbm, out_hbm, near_ref, terms_ref, out_ref, in_sems, out_sems):
-    half = arrived_ref.shape[0]
+def upper_half(words):
+    return (words >> 16).astype(F32)
+
+
+def lower_half(words):
+    return ((words << 16) >> 16).astype(F32)
+
+
+def loose_values(arrived_ref):
+    words = arrived_ref[:, LANES:]
+    low_lanes = lane_ids(words.shape) < PANEL
+    scale = jnp.exp2(((words & 255) - (BIAS + 15)).astype(F32)) * (1 / MARGIN)
+    other = swap_halves(scale)
+    near = upper_half(words) * scale
+    words = arrived_ref[:, :LANES]
+    low = upper_half(words) * jnp.where(low_lanes, scale, other)
+    return low, lower_half(words) * jnp.where(low_lanes, other, scale), near
+
+
+def tight_values(arrived_ref, part_rows, values_ref):
+    first = tight_split(part_rows)
+    second = part_rows - first
+    step = part_rows + first
+    sources = arrived_ref.shape[0] // step
+    pairs = [arrived_ref[i * step + part_rows + second : i * step + part_rows + second + 2, :] for i in range(sources)]
+    spare = jnp.zeros((LANES - 2 * sources, LANES), jnp.int32)
+    exponents = jnp.concatenate([*pairs, spare], axis=0)
+    scales = jnp.exp2(jnp.transpose(exponents.astype(F32)) - 15.0) * (1 / MARGIN)
+    scales = scales[PANEL : PANEL + part_rows]
+    low_lanes = lane_ids((part_rows, LANES)) < PANEL
+    for i in range(sources):
+        base = i * step
+        here = slice(i * part_rows, (i + 1) * part_rows)
+        low_scale = jnp.broadcast_to(scales[:, 2 * i : 2 * i + 1], (part_rows, LANES))
+        high_scale = jnp.broadcast_to(scales[:, 2 * i + 1 : 2 * i + 2], (part_rows, LANES))
+        words = arrived_ref[base : base + part_rows, :]
+        values_ref[0, here, :] = upper_half(words) * low_scale
+        values_ref[1, here, :] = lower_half(words) * high_scale
+        words = arrived_ref[base + part_rows : base + step, :]
+        words = jnp.concatenate([words, swap_halves(words[:second])], axis=0)
+        words = jnp.where(low_lanes, words, swap_halves(words))
+        values_ref[2, here, :] = jnp.where(low_lanes, upper_half(words) * low_scale, lower_half(words) * high_scale)
+    return values_ref[0], values_ref[1], values_ref[2]
+
+
+def formed_kernel(
+    part_rows, index_ref, arrived_ref, near_hbm, out_hbm, near_ref, terms_ref, out_ref, values_ref, in_sems, out_sems
+):
+    half = terms_ref.shape[0] // 2
+    first = tight_split(part_rows)
     block = A_BLOCK
     starts = range(0, near_ref.shape[0], block)
 
@@ -516,20 +602,15 @@
     ]
     for fetch in fetches:
         fetch.start()
-    words = arrived_ref[:, LANES:]
-    low_lanes = lane_ids(words.shape) < PANEL
-    scale = jnp.exp2(((words & 255) - (BIAS + 15)).astype(F32)) * (1 / MARGIN)
-    other = swap_halves(scale)
-    first, second = (term.astype(F32) for term in split((words >> 16).astype(F32) * scale, 2))
-    terms_ref[:half, 2 * LANES :] = jnp.where(low_lanes, first, swap_halves(second)).astype(BF16)
-    terms_ref[half:, 2 * LANES :] = jnp.where(low_lanes, swap_halves(first), second).astype(BF16)
-    words = arrived_ref[:, :LANES]
-    low = (words >> 16).astype(F32) * jnp.where(low_lanes, scale, other)
-    high = ((words << 16) >> 16).astype(F32) * jnp.where(low_lanes, other, scale)
+    low, high, near = loose_values(arrived_ref) if not first else tight_values(arrived_ref, part_rows, values_ref)
     for side, values in enumerate((low, high)):
-        first, second = split(values, 2)
-        terms_ref[side * half : (side + 1) * half, :LANES] = first
-        terms_ref[side * half : (side + 1) * half, LANES : 2 * LANES] = second
+        one, two = split(values, 2)
+        terms_ref[side * half : (side + 1) * half, :LANES] = one
+        terms_ref[side * half : (side + 1) * half, LANES : 2 * LANES] = two
+    low_lanes = lane_ids(near.shape) < PANEL
+    one, two = (term.astype(F32) for term in split(near, 2))
+    terms_ref[:half, 2 * LANES :] = jnp.where(low_lanes, one, swap_halves(two)).astype(BF16)
+    terms_ref[half:, 2 * LANES :] = jnp.where(low_lanes, swap_halves(one), two).astype(BF16)
 
     stores = []
     for i, start in enumerate(starts):
@@ -550,12 +631,12 @@
         store.wait()
 
 
-def formed_columns(index, arrived, near):
+def formed_columns(index, arrived, near, part_rows):
     rows, columns = near.shape
     vmem = pl.BlockSpec(memory_space=pltpu.VMEM)
     anywhere = pl.BlockSpec(memory_space=pltpu.HBM)
     return pl.pallas_call(
-        formed_kernel,
+        functools.partial(formed_kernel, part_rows),
         in_specs=[vmem, vmem, anywhere],
         out_specs=anywhere,
         out_shape=pltpu.HBM((rows, columns), F32),
@@ -564,6 +645,7 @@
             pltpu.VMEM((rows, columns), F32),
             pltpu.VMEM((rows, 3 * LANES), BF16),
             pltpu.VMEM((rows, columns), F32),
+            pltpu.VMEM((3, rows // 2, LANES), F32),
             pltpu.SemaphoreType.DMA((rows // A_BLOCK,)),
             pltpu.SemaphoreType.DMA((rows // A_BLOCK,)),
         ],
@@ -623,7 +705,9 @@
             later_parts = exchange(tied(rest_parts[1:], *leading_parts), apart[-1], "wide")
     late = len(later_parts) // 2
     rest_parts = rest_parts + other_parts + later_parts[late:]
-    rest_out = rest_products(my_index, order, a_rows, rest_parts, offsets_of(apart), packing)
+    rest_out = rest_products(
+        my_index, order, a_rows, rest_parts, offsets_of(apart), packing, share // 2
+    )
     rest_in = swap_rows(tied([rest_out], *leading_parts)[0], group)
     near, updated, pivots = updates(
         my_index,
@@ -636,7 +720,7 @@
         blocks_held,
         columns,
     )
-    factored = formed_columns(index, rest_in, near)
+    factored = formed_columns(index, rest_in, near, share // 2)
     return (factored, updated, pivots[0])
 
 

time: 81.9 us -> 80.1 us (0.978)
  waiting for transfers between devices: 21.3 us -> 19.1 us
    all_to_all x2, waiting for transfers between devices: 13.6 us -> 11.5 us  [swap_rows(): lax.all_to_all(x.reshape(group, rows // group, width), 'wide', split_axis...]
where the time goes in v1:
time: 80.1 us; the launch traced here: 79.6 us
  Pallas kernels  30.9 us (39%)
  starting transfers between devices  28.4 us (35%)
  waiting for transfers between devices  19.1 us (24%)
  between operations  0.97 us (1%)
    ppermute x17, starting transfers between devices, exchange(): lax.ppermute(part, axis, [(i, i ^ mask) for i in range(size)])  20 us
    pallas_call x1, Pallas kernels, updates(): pl.pallas_call(functools.partial(update_kernel, offsets, blocks_held, col...  12 us
    all_to_all x2, waiting for transfers between devices, swap_rows(): lax.all_to_all(x.reshape(group, rows // group, width), 'wide', split_axis...  11.5 us
    all_to_all x2, starting transfers between devices, swap_rows(): lax.all_to_all(x.reshape(group, rows // group, width), 'wide', split_axis...  8.36 us
    ppermute x17, waiting for transfers between devices, exchange(): lax.ppermute(part, axis, [(i, i ^ mask) for i in range(size)])  7.68 us
    pallas_call x1, Pallas kernels, rest_products(): pl.pallas_call(functools.partial(rest_product_kernel, offsets, share, par...  7.5 us
    pallas_call x1, Pallas kernels, formed_columns(): pl.pallas_call(functools.partial(formed_kernel, part_rows), in_specs=[vme...  4.15 us
    pallas_call x1, Pallas kernels, lead_products(): pl.pallas_call(functools.partial(lead_product_kernel, offsets), in_specs=...  3.23 us
  transfers between devices with their start and end apart: 19, of which 9 were waited for; matrix products, arithmetic and copies ran while one was open for 0% of the time, Pallas kernels for 32%

profile of v1, /device:TPU:0, one launch (start us, length us, event | category | flops | bytes accessed | tf_op | source)
XLA Modules:
  0.0 79.6 jit_solution(7293521689492223155)
XLA Ops:
  0.6 1.0 %split_panels.1 = (bf16[1,128,128]{2,1,0:T(8,128)(2,1)S(1)}, bf16[1,128,384]{2,1,0:T(8,128)(2,1)S(1)}) custom-call(s32[1]{0:T(128)} %bitcast.my_ref, bf16[128,256]{1,0:T(8,128)(2,1)} %xa_hbm.1, bf16[128,256]{1,0:T(8,128)(2,1)} %za_hbm.1), custom_call_target="tpu_custom_call" | custom-call | tf_op jit(solution)/shard_map/split_panels/pallas_call | solution.py:167
  1.6 4.1 %collective-permute-start.2 = (bf16[1,128,128]{2,1,0:T(8,128)(2,1)S(1)}, bf16[1,128,128]{2,1,0:T(8,128)(2,1)S(1)}, u32[]{:S(2)}, u32[]{:S(2)}) collective-permute-start(bf16[1,128,128]{2,1,0:T(8,128)(2,1)S(1)} %get-tuple-element.23), channel_id=1, source_target_pairs={{0,8},{1,9},{2,10},{3,11},{4,12},{5,13},{6,14},{7,15},{8,0},{9,1},... | collective-permute-start | bytes 98312 | tf_op jit(solution)/shard_map/ppermute | solution.py:94
  5.7 1.6 %collective-permute-start.3 = (bf16[1,128,128]{2,1,0:T(8,128)(2,1)S(1)}, bf16[1,128,128]{2,1,0:T(8,128)(2,1)S(1)}, u32[]{:S(2)}, u32[]{:S(2)}) collective-permute-start(bf16[1,128,128]{2,1,0:T(8,128)(2,1)S(1)} %get-tuple-element.23), channel_id=1, source_target_pairs={{0,4},{1,5},{2,6},{3,7},{4,0},{5,1},{6,2},{7,3},{8,12},{9,13},{10,... | collective-permute-start | bytes 98312 | tf_op jit(solution)/shard_map/ppermute | solution.py:94
  7.3 1.9 %collective-permute-start = (bf16[1,128,384]{2,1,0:T(8,128)(2,1)S(1)}, bf16[1,128,384]{2,1,0:T(8,128)(2,1)S(1)}, u32[]{:S(2)}, u32[]{:S(2)}) collective-permute-start(bf16[1,128,384]{2,1,0:T(8,128)(2,1)S(1)} %get-tuple-element.20), channel_id=1, source_target_pairs={{0,8},{1,9},{2,10},{3,11},{4,12},{5,13},{6,14},{7,15},{8,0},{9,1},... | collective-permute-start | bytes 294920 | tf_op jit(solution)/shard_map/ppermute | solution.py:94
  9.3 0.4 collective-permute-done.3
  9.7 3.4 %collective-permute-done.4 = bf16[1,128,128]{2,1,0:T(8,128)(2,1)S(1)} collective-permute-done((bf16[1,128,128]{2,1,0:T(8,128)(2,1)S(1)}, bf16[1,128,128]{2,1,0:T(8,128)(2,1)S(1)}, u32[]{:S(2)}, u32[]{:S(2)}) %collective-permute-start.4) | collective-permute-done | bytes 32800 | tf_op jit(solution)/shard_map/ppermute | solution.py:94
  13.0 1.5 %collective-permute-start.5 = (bf16[4,128,128]{2,1,0:T(8,128)(2,1)S(1)}, bf16[4,128,128]{2,1,0:T(8,128)(2,1)S(1)}, u32[]{:S(2)}, u32[]{:S(2)}) collective-permute-start(bf16[4,128,128]{2,1,0:T(8,128)(2,1)S(1)} %constant_dynamic-update-slice_fusion.2.refs_0_), channel_id=1, source_target_pairs={{0,2},{1,3},{2,0},{3,1},{4,6},{5,7},{6,4},{7,5},{8,10},{9,11},{10,... | collective-permute-start | bytes 393224 | tf_op jit(solution)/shard_map/ppermute | solution.py:94
  14.6 0.6 collective-permute-start.7
  15.2 0.2 collective-permute-done
  15.4 1.7 %collective-permute-start.1 = (bf16[2,128,384]{2,1,0:T(8,128)(2,1)S(1)}, bf16[2,128,384]{2,1,0:T(8,128)(2,1)S(1)}, u32[]{:S(2)}, u32[]{:S(2)}) collective-permute-start(bf16[2,128,384]{2,1,0:T(8,128)(2,1)S(1)} %constant_dynamic-update-slice_fusion), channel_id=1, source_target_pairs={{0,4},{1,5},{2,6},{3,7},{4,0},{5,1},{6,2},{7,3},{8,12},{9,13},{10,... | collective-permute-start | bytes 589832 | tf_op jit(solution)/shard_map/ppermute | solution.py:94
  17.0 2.5 %order_picks.1 = (bf16[1280,1280]{1,0:T(8,128)(2,1)S(1)}, bf16[1280,2048]{1,0:T(8,128)(2,1)S(1)}) custom-call(s32[1,1280]{1,0:T(1,128)} %order_ref.1, bf16[1280,2048]{1,0:T(8,128)(2,1)} %a_hbm.3), custom_call_target="tpu_custom_call" | custom-call | flops 6553600 | bytes 10485760 | tf_op jit(solution)/shard_map/order_picks/pallas_call | solution.py:134
  19.6 0.8 collective-permute-done.7.refs_3_
  20.3 3.2 %lead_products.1 = f32[640,128]{1,0:T(8,128)} custom-call(s32[1]{0:T(128)} %bitcast.my_ref, bf16[1280,2048]{1,0:T(8,128)(2,1)S(1)} %get-tuple-element.21.a_ref, bf16[1280,1280]{1,0:T(8,128)(2,1)S(1)} %get-tuple-element.22.picks_ref, bf16[4,128,128]{2,1,0:T(8,128)(2,1)S(1)} %constant_dynamic-update-slice_fusion.2.refs_0_, ...), custom_call_target="tpu_custom_call" | custom-call | flops 1509949440 | bytes 5242880 | tf_op jit(solution)/shard_map/lead_products/pallas_call | solution.py:220
  23.6 4.2 %all-to-all-start = ((f32[16,40,128]{2,1,0:T(8,128)}), f32[16,40,128]{2,1,0:T(8,128)S(1)}, u32[]{:S(2)}, u32[]{:S(2)}) async-start(f32[16,40,128]{2,1,0:T(8,128)} %bitcast.1), calls=%async_computation | async-start | bytes 655360 | tf_op jit(solution)/shard_map/all_to_all | solution.py:662
  27.9 2.0 %collective-permute-start.8 = (bf16[4,128,384]{2,1,0:T(8,128)(2,1)S(1)}, bf16[4,128,384]{2,1,0:T(8,128)(2,1)S(1)}, u32[]{:S(2)}, u32[]{:S(2)}) collective-permute-start(bf16[4,128,384]{2,1,0:T(8,128)(2,1)S(1)} %constant_dynamic-update-slice_fusion.6.refs_0_), channel_id=1, source_target_pairs={{0,2},{1,3},{2,0},{3,1},{4,6},{5,7},{6,4},{7,5},{8,10},{9,11},{10,... | collective-permute-start | bytes 1179656 | tf_op jit(solution)/shard_map/ppermute | solution.py:94
  29.9 0.1 fusion.index_ref
  30.0 9.0 %all-to-all-done = f32[16,40,128]{2,1,0:T(8,128)S(1)} async-done(((f32[16,40,128]{2,1,0:T(8,128)}), f32[16,40,128]{2,1,0:T(8,128)S(1)}, u32[]{:S(2)}, u32[]{:S(2)}) %all-to-all-start) | async-done | bytes 327712 | tf_op jit(solution)/shard_map/all_to_all | solution.py:662
  38.9 0.5 leading_rows.1
  39.5 1.6 %collective-permute-start.10 = (f32[1,64,128]{2,1,0:T(8,128)S(1)}, f32[1,64,128]{2,1,0:T(8,128)S(1)}, u32[]{:S(2)}, u32[]{:S(2)}) collective-permute-start(f32[1,64,128]{2,1,0:T(8,128)S(1)} %leading_rows.1), channel_id=1, source_target_pairs={{0,8},{1,9},{2,10},{3,11},{4,12},{5,13},{6,14},{7,15},{8,0},{9,1},... | collective-permute-start | bytes 98312 | tf_op jit(solution)/shard_map/ppermute | solution.py:94
  41.0 0.2 collective-permute-start.11
  41.2 2.7 %collective-permute-start.12 = (f32[1,64,128]{2,1,0:T(8,128)S(1)}, f32[1,64,128]{2,1,0:T(8,128)S(1)}, u32[]{:S(2)}, u32[]{:S(2)}) collective-permute-start(f32[1,64,128]{2,1,0:T(8,128)S(1)} %leading_rows.1), channel_id=1, source_target_pairs={{0,12},{1,13},{2,14},{3,15},{4,8},{5,9},{6,10},{7,11},{8,4},{9,5},... | collective-permute-start | bytes 98312 | tf_op jit(solution)/shard_map/ppermute | solution.py:94
  44.0 1.0 %collective-permute-done.10 = f32[1,64,128]{2,1,0:T(8,128)S(1)} collective-permute-done((f32[1,64,128]{2,1,0:T(8,128)S(1)}, f32[1,64,128]{2,1,0:T(8,128)S(1)}, u32[]{:S(2)}, u32[]{:S(2)}) %collective-permute-start.10) | collective-permute-done | bytes 32800 | tf_op jit(solution)/shard_map/ppermute | solution.py:94
  45.0 0.2 collective-permute-done.11
  45.1 1.8 %collective-permute-done.12 = f32[1,64,128]{2,1,0:T(8,128)S(1)} collective-permute-done((f32[1,64,128]{2,1,0:T(8,128)S(1)}, f32[1,64,128]{2,1,0:T(8,128)S(1)}, u32[]{:S(2)}, u32[]{:S(2)}) %collective-permute-start.12) | collective-permute-done | bytes 32800 | tf_op jit(solution)/shard_map/ppermute | solution.py:94
  47.0 1.4 %collective-permute-start.14 = (f32[4,64,128]{2,1,0:T(8,128)S(1)}, f32[4,64,128]{2,1,0:T(8,128)S(1)}, u32[]{:S(2)}, u32[]{:S(2)}) collective-permute-start(f32[4,64,128]{2,1,0:T(8,128)S(1)} %pad_maximum_fusion.refs_0_), channel_id=1, source_target_pairs={{0,2},{1,3},{2,0},{3,1},{4,6},{5,7},{6,4},{7,5},{8,10},{9,11},{10,... | collective-permute-start | bytes 393224 | tf_op jit(solution)/shard_map/ppermute | solution.py:94
  48.3 0.2 collective-permute-start.15
  48.6 0.6 collective-permute-start.16
  49.2 7.5 %rest_products.1 = s32[1024,128]{1,0:T(8,128)} custom-call(s32[1]{0:T(128)} %bitcast.my_ref, s32[1,1280]{1,0:T(1,128)S(1)} %copy-done, bf16[1280,2048]{1,0:T(8,128)(2,1)} %a_hbm.3, bf16[4,128,384]{2,1,0:T(8,128)(2,1)S(1)} %constant_dynamic-update-slice_fusion.6.refs_0_, bf16[4,128,384]{2,1,0:T(8,128)(2,1)S(1)} %collective-permute-done.8.refs_1_, ...), custom_call_target="tpu_custom_call" | custom-call | flops 3690987520 | bytes 5242880 | tf_op jit(solution)/shard_map/rest_products/pallas_call | solution.py:343
  56.7 4.1 %all-to-all-start.1 = ((s32[16,64,128]{2,1,0:T(8,128)}), s32[16,64,128]{2,1,0:T(8,128)S(1)}, u32[]{:S(2)}, u32[]{:S(2)}) async-start(s32[16,64,128]{2,1,0:T(8,128)} %bitcast.3), calls=%async_computation.1 | async-start | bytes 1048576 | tf_op jit(solution)/shard_map/all_to_all | solution.py:662
  60.9 12.0 %factor_and_update.1 = (f32[1280,256]{1,0:T(8,128)}, bf16[1280,1024]{1,0:T(8,128)(2,1)}, f32[1,64]{1,0:T(1,128)}) custom-call(s32[1]{0:T(128)} %bitcast.my_ref, s32[1,1280]{1,0:T(1,128)S(1)} %fusion.index_ref, f32[640,128]{1,0:T(8,128)S(1)} %bitcast.8, f32[1,64]{1,0:T(1,128)S(1)} %bitcast.10, bf16[1280,1024]{1,0:T(8,128)(2,1)} %resident_hbm.1, ...), custom_call_target="tpu_custom_call" | custom-call | flops 838860800 | bytes 6553600 | tf_op jit(solution)/shard_map/factor_and_update/pallas_call | solution.py:515
  72.8 2.5 %all-to-all-done.1 = s32[16,64,128]{2,1,0:T(8,128)S(1)} async-done(((s32[16,64,128]{2,1,0:T(8,128)}), s32[16,64,128]{2,1,0:T(8,128)S(1)}, u32[]{:S(2)}, u32[]{:S(2)}) %all-to-all-start.1) | async-done | bytes 524320 | tf_op jit(solution)/shard_map/all_to_all | solution.py:662
  75.3 4.1 %formed_columns.1 = f32[1280,256]{1,0:T(8,128)} custom-call(s32[1,1280]{1,0:T(1,128)S(1)} %fusion.index_ref, s32[1024,128]{1,0:T(8,128)S(1)} %bitcast.9, f32[1280,256]{1,0:T(8,128)} %get-tuple-element.34.near_hbm), custom_call_target="tpu_custom_call", output_to_operand_aliasing={{}: (2, {})} | custom-call | flops 1677721600 | bytes 2621440 | tf_op jit(solution)/shard_map/formed_columns/pallas_call | solution.py:638
  (29 shorter events, 0.2 us)
Async XLA Ops:
  1.6 7.6 %collective-permute-start.2 = (bf16[1,128,128]{2,1,0:T(8,128)(2,1)S(1)}, bf16[1,128,128]{2,1,0:T(8,128)(2,1)S(1)}, u32[]{:S(2)}, u32[]{:S(2)}) collective-permute-start(bf16[1,128,128]{2,1,0:T(8,128)(2,1)S(1)} %get-tuple-element.23), channel_id=1, source_target_pairs={{0,8},{1,9},{2,10},{3,11},{4,12},{5,13},{6,14},{7,15},{8,0},{9,1},... | collective-permute-start | bytes 98312 | tf_op jit(solution)/shard_map/ppermute | solution.py:94
  5.7 3.9 %collective-permute-start.3 = (bf16[1,128,128]{2,1,0:T(8,128)(2,1)S(1)}, bf16[1,128,128]{2,1,0:T(8,128)(2,1)S(1)}, u32[]{:S(2)}, u32[]{:S(2)}) collective-permute-start(bf16[1,128,128]{2,1,0:T(8,128)(2,1)S(1)} %get-tuple-element.23), channel_id=1, source_target_pairs={{0,4},{1,5},{2,6},{3,7},{4,0},{5,1},{6,2},{7,3},{8,12},{9,13},{10,... | collective-permute-start | bytes 98312 | tf_op jit(solution)/shard_map/ppermute | solution.py:94
  7.3 5.7 %collective-permute-start.4 = (bf16[1,128,128]{2,1,0:T(8,128)(2,1)S(1)}, bf16[1,128,128]{2,1,0:T(8,128)(2,1)S(1)}, u32[]{:S(2)}, u32[]{:S(2)}) collective-permute-start(bf16[1,128,128]{2,1,0:T(8,128)(2,1)S(1)} %get-tuple-element.23), channel_id=1, source_target_pairs={{0,12},{1,13},{2,14},{3,15},{4,8},{5,9},{6,10},{7,11},{8,4},{9,5},... | collective-permute-start | bytes 98312 | tf_op jit(solution)/shard_map/ppermute | solution.py:94
  7.3 8.0 %collective-permute-start = (bf16[1,128,384]{2,1,0:T(8,128)(2,1)S(1)}, bf16[1,128,384]{2,1,0:T(8,128)(2,1)S(1)}, u32[]{:S(2)}, u32[]{:S(2)}) collective-permute-start(bf16[1,128,384]{2,1,0:T(8,128)(2,1)S(1)} %get-tuple-element.20), channel_id=1, source_target_pairs={{0,8},{1,9},{2,10},{3,11},{4,12},{5,13},{6,14},{7,15},{8,0},{9,1},... | collective-permute-start | bytes 294920 | tf_op jit(solution)/shard_map/ppermute | solution.py:94
  13.0 6.5 %collective-permute-start.5 = (bf16[4,128,128]{2,1,0:T(8,128)(2,1)S(1)}, bf16[4,128,128]{2,1,0:T(8,128)(2,1)S(1)}, u32[]{:S(2)}, u32[]{:S(2)}) collective-permute-start(bf16[4,128,128]{2,1,0:T(8,128)(2,1)S(1)} %constant_dynamic-update-slice_fusion.2.refs_0_), channel_id=1, source_target_pairs={{0,2},{1,3},{2,0},{3,1},{4,6},{5,7},{6,4},{7,5},{8,10},{9,11},{10,... | collective-permute-start | bytes 393224 | tf_op jit(solution)/shard_map/ppermute | solution.py:94
  14.6 5.0 %collective-permute-start.6 = (bf16[4,128,128]{2,1,0:T(8,128)(2,1)S(1)}, bf16[4,128,128]{2,1,0:T(8,128)(2,1)S(1)}, u32[]{:S(2)}, u32[]{:S(2)}) collective-permute-start(bf16[4,128,128]{2,1,0:T(8,128)(2,1)S(1)} %constant_dynamic-update-slice_fusion.2.refs_0_), channel_id=1, source_target_pairs={{0,1},{1,0},{2,3},{3,2},{4,5},{5,4},{6,7},{7,6},{8,9},{9,8},{10,11... | collective-permute-start | bytes 393224 | tf_op jit(solution)/shard_map/ppermute | solution.py:94
  14.6 5.8 %collective-permute-start.7 = (bf16[4,128,128]{2,1,0:T(8,128)(2,1)S(1)}, bf16[4,128,128]{2,1,0:T(8,128)(2,1)S(1)}, u32[]{:S(2)}, u32[]{:S(2)}) collective-permute-start(bf16[4,128,128]{2,1,0:T(8,128)(2,1)S(1)} %constant_dynamic-update-slice_fusion.2.refs_0_), channel_id=1, source_target_pairs={{0,3},{1,2},{2,1},{3,0},{4,7},{5,6},{6,5},{7,4},{8,11},{9,10},{10,... | collective-permute-start | bytes 393224 | tf_op jit(solution)/shard_map/ppermute | solution.py:94
  15.4 8.2 %collective-permute-start.1 = (bf16[2,128,384]{2,1,0:T(8,128)(2,1)S(1)}, bf16[2,128,384]{2,1,0:T(8,128)(2,1)S(1)}, u32[]{:S(2)}, u32[]{:S(2)}) collective-permute-start(bf16[2,128,384]{2,1,0:T(8,128)(2,1)S(1)} %constant_dynamic-update-slice_fusion), channel_id=1, source_target_pairs={{0,4},{1,5},{2,6},{3,7},{4,0},{5,1},{6,2},{7,3},{8,12},{9,13},{10,... | collective-permute-start | bytes 589832 | tf_op jit(solution)/shard_map/ppermute | solution.py:94
  20.3 9.5 %copy-start.2 = (s32[1,1280]{1,0:T(1,128)S(1)}, s32[1,1280]{1,0:T(1,128)}, u32[]{:S(2)}) copy-start(s32[1,1280]{1,0:T(1,128)} %param.11) | copy-start | bytes 15364
  20.3 28.8 %copy-start = (s32[1,1280]{1,0:T(1,128)S(1)}, s32[1,1280]{1,0:T(1,128)}, u32[]{:S(2)}) copy-start(s32[1,1280]{1,0:T(1,128)} %order_ref.1) | copy-start | bytes 15364
  23.6 15.4 %all-to-all-start = ((f32[16,40,128]{2,1,0:T(8,128)}), f32[16,40,128]{2,1,0:T(8,128)S(1)}, u32[]{:S(2)}, u32[]{:S(2)}) async-start(f32[16,40,128]{2,1,0:T(8,128)} %bitcast.1), calls=%async_computation | async-start | bytes 655360 | tf_op jit(solution)/shard_map/all_to_all | solution.py:662
  27.9 16.1 %collective-permute-start.8 = (bf16[4,128,384]{2,1,0:T(8,128)(2,1)S(1)}, bf16[4,128,384]{2,1,0:T(8,128)(2,1)S(1)}, u32[]{:S(2)}, u32[]{:S(2)}) collective-permute-start(bf16[4,128,384]{2,1,0:T(8,128)(2,1)S(1)} %constant_dynamic-update-slice_fusion.6.refs_0_), channel_id=1, source_target_pairs={{0,2},{1,3},{2,0},{3,1},{4,6},{5,7},{6,4},{7,5},{8,10},{9,11},{10,... | collective-permute-start | bytes 1179656 | tf_op jit(solution)/shard_map/ppermute | solution.py:94
  39.5 5.5 %collective-permute-start.10 = (f32[1,64,128]{2,1,0:T(8,128)S(1)}, f32[1,64,128]{2,1,0:T(8,128)S(1)}, u32[]{:S(2)}, u32[]{:S(2)}) collective-permute-start(f32[1,64,128]{2,1,0:T(8,128)S(1)} %leading_rows.1), channel_id=1, source_target_pairs={{0,8},{1,9},{2,10},{3,11},{4,12},{5,13},{6,14},{7,15},{8,0},{9,1},... | collective-permute-start | bytes 98312 | tf_op jit(solution)/shard_map/ppermute | solution.py:94
  41.0 4.1 %collective-permute-start.11 = (f32[1,64,128]{2,1,0:T(8,128)S(1)}, f32[1,64,128]{2,1,0:T(8,128)S(1)}, u32[]{:S(2)}, u32[]{:S(2)}) collective-permute-start(f32[1,64,128]{2,1,0:T(8,128)S(1)} %leading_rows.1), channel_id=1, source_target_pairs={{0,4},{1,5},{2,6},{3,7},{4,0},{5,1},{6,2},{7,3},{8,12},{9,13},{10,... | collective-permute-start | bytes 98312 | tf_op jit(solution)/shard_map/ppermute | solution.py:94
  41.2 5.7 %collective-permute-start.12 = (f32[1,64,128]{2,1,0:T(8,128)S(1)}, f32[1,64,128]{2,1,0:T(8,128)S(1)}, u32[]{:S(2)}, u32[]{:S(2)}) collective-permute-start(f32[1,64,128]{2,1,0:T(8,128)S(1)} %leading_rows.1), channel_id=1, source_target_pairs={{0,12},{1,13},{2,14},{3,15},{4,8},{5,9},{6,10},{7,11},{8,4},{9,5},... | collective-permute-start | bytes 98312 | tf_op jit(solution)/shard_map/ppermute | solution.py:94
  43.9 5.2 %collective-permute-start.9 = (bf16[4,128,384]{2,1,0:T(8,128)(2,1)S(1)}, bf16[4,128,384]{2,1,0:T(8,128)(2,1)S(1)}, u32[]{:S(2)}, u32[]{:S(2)}) collective-permute-start(bf16[4,128,384]{2,1,0:T(8,128)(2,1)S(1)} %constant_dynamic-update-slice_fusion.6.refs_0_), channel_id=1, source_target_pairs={{0,1},{1,0},{2,3},{3,2},{4,5},{5,4},{6,7},{7,6},{8,9},{9,8},{10,11... | collective-permute-start | bytes 1179656 | tf_op jit(solution)/shard_map/ppermute | solution.py:94
  46.9 2.2 %collective-permute-start.13 = (bf16[4,128,384]{2,1,0:T(8,128)(2,1)S(1)}, bf16[4,128,384]{2,1,0:T(8,128)(2,1)S(1)}, u32[]{:S(2)}, u32[]{:S(2)}) collective-permute-start(bf16[4,128,384]{2,1,0:T(8,128)(2,1)S(1)} %collective-permute-done.8.refs_1_), channel_id=1, source_target_pairs={{0,1},{1,0},{2,3},{3,2},{4,5},{5,4},{6,7},{7,6},{8,9},{9,8},{10,11... | collective-permute-start | bytes 1179656 | tf_op jit(solution)/shard_map/ppermute | solution.py:94
  46.9 13.9 %copy-start.1 = (f32[64]{0:T(128)S(1)}, f32[64]{0:T(128)}, u32[]{:S(2)}) copy-start(f32[64]{0:T(128)} %param.12) | copy-start | bytes 772
  47.0 9.7 %collective-permute-start.14 = (f32[4,64,128]{2,1,0:T(8,128)S(1)}, f32[4,64,128]{2,1,0:T(8,128)S(1)}, u32[]{:S(2)}, u32[]{:S(2)}) collective-permute-start(f32[4,64,128]{2,1,0:T(8,128)S(1)} %pad_maximum_fusion.refs_0_), channel_id=1, source_target_pairs={{0,2},{1,3},{2,0},{3,1},{4,6},{5,7},{6,4},{7,5},{8,10},{9,11},{10,... | collective-permute-start | bytes 393224 | tf_op jit(solution)/shard_map/ppermute | solution.py:94
  48.3 8.4 %collective-permute-start.15 = (f32[4,64,128]{2,1,0:T(8,128)S(1)}, f32[4,64,128]{2,1,0:T(8,128)S(1)}, u32[]{:S(2)}, u32[]{:S(2)}) collective-permute-start(f32[4,64,128]{2,1,0:T(8,128)S(1)} %pad_maximum_fusion.refs_0_), channel_id=1, source_target_pairs={{0,1},{1,0},{2,3},{3,2},{4,5},{5,4},{6,7},{7,6},{8,9},{9,8},{10,11... | collective-permute-start | bytes 393224 | tf_op jit(solution)/shard_map/ppermute | solution.py:94
  48.6 8.1 %collective-permute-start.16 = (f32[4,64,128]{2,1,0:T(8,128)S(1)}, f32[4,64,128]{2,1,0:T(8,128)S(1)}, u32[]{:S(2)}, u32[]{:S(2)}) collective-permute-start(f32[4,64,128]{2,1,0:T(8,128)S(1)} %pad_maximum_fusion.refs_0_), channel_id=1, source_target_pairs={{0,3},{1,2},{2,1},{3,0},{4,7},{5,6},{6,5},{7,4},{8,11},{9,10},{10,... | collective-permute-start | bytes 393224 | tf_op jit(solution)/shard_map/ppermute | solution.py:94
  56.7 18.6 %all-to-all-start.1 = ((s32[16,64,128]{2,1,0:T(8,128)}), s32[16,64,128]{2,1,0:T(8,128)S(1)}, u32[]{:S(2)}, u32[]{:S(2)}) async-start(s32[16,64,128]{2,1,0:T(8,128)} %bitcast.3), calls=%async_computation.1 | async-start | bytes 1048576 | tf_op jit(solution)/shard_map/all_to_all | solution.py:662
